TPU v7x, 32 devices: a whole 2x2x4 slice. The times are simulated.
32 devices in a mesh: group: 4 (over y, core), blk: 8 (over z, x).
Axes of the slice: x: 2, y: 2, z: 4, core: 2. Of those that a mesh axis runs over, the one named last changes fastest.
Arguments:
- queries: bfloat16 [2048, 32, 128], P('blk'), may hold values from -8 to 8
- doc_blocks: bfloat16 [4, 128, 128, 128], P('group', 'blk'), may hold values from -2 to 2
- doc_len: int32 [4, 128], P('group', 'blk'), may hold values from 96 to 128
- candidates: int32 [4, 8, 4, 8], P('group', 'blk'), may hold values from 0 to 17, as said below
- cand_count: int32 [4, 8, 4], P('group', 'blk'), may hold values from 2 to 8, as said below
- hot_owned: int32 [4, 8, 1], P('group', 'blk'), may hold values from 0 to 15
- hot_taken: int32 [4, 8, 2], P('group', 'blk'), may hold values from 0 to 7, as said below
Outputs:
- top_scores: float32 [2048, 16], P('blk')
Inputs may be any that keep to these rules, and one draw needn't show every extreme that they name: `candidates`: slots below 16 name a device's own blocks, the others its hot copies; entries at or past the hop's count are ignored. `cand_count`: every query block has 8 live candidates at one or more of its hops. `hot_taken`: entries are hot pool indices of the same group; every pool entry is held by some device.
All inputs are finite; a program needn't handle non-finite values.
Results may differ from a plain program's by a relative error of at most 0.0003.
Values may be sent and summed in bfloat16 or wider, within the bound.
A program may use at most 64 MiB of HBM per device.

v0:
```python
import jax
import jax.numpy as jnp
from jax import lax
from jax.sharding import PartitionSpec as P

QTOK = 32
TOPK = 16
MASKED_SCORE = -1e30


def shifted(x, axis, by):
    peers = lax.axis_size(axis)
    return lax.ppermute(x, axis, [(i, (i + by) % peers) for i in range(peers)])


def maxsim(query_part, blocks, lengths):

    def single(element):
        doc_block, length = element
        scores = lax.dot_general(
            query_part, doc_block, (((1,), (1,)), ((), ())), preferred_element_type=jnp.float32
        )
        keep_mask = jnp.arange(doc_block.shape[0], dtype=jnp.int32) < length
        scores = jnp.where(keep_mask[None, :], scores, MASKED_SCORE)
        best_rows = jnp.max(scores, axis=1).reshape(-1, QTOK)
        return jnp.sum(best_rows, axis=1) / QTOK

    return lax.map(single, (blocks, lengths)).T


def masked_scores(query_part, chosen, chosen_len, live_count):
    scores = maxsim(query_part, chosen, chosen_len)
    keep_mask = jnp.arange(chosen.shape[0], dtype=jnp.int32) < live_count
    return jnp.where(keep_mask[None, :], scores, MASKED_SCORE)


def hop_scores(query_part, blocks, lengths, slots, live_count):
    chosen = jnp.take(blocks, slots, axis=0)
    chosen_len = jnp.take(lengths, slots, axis=0)
    return masked_scores(query_part, chosen, chosen_len, live_count)


def on_device(queries, doc_blocks, doc_len, candidates, cand_count, hot_owned, hot_taken):
    lengths_all, cand_all, count_all, taken_all, owned_all = (
        lax.all_gather(doc_len, "blk", axis=1, tiled=True),
        lax.all_gather(candidates, "blk", axis=1, tiled=True),
        lax.all_gather(cand_count, "blk", axis=1, tiled=True),
        lax.all_gather(hot_taken, "blk", axis=1, tiled=True),
        lax.all_gather(hot_owned, "blk", axis=1, tiled=True),
    )
    shards = lax.axis_size("blk")
    position = lax.axis_index("blk")
    per_dev = doc_blocks.shape[1]
    hot_pub = hot_owned.shape[2]
    hot_dev = hot_taken.shape[2]
    hop_total = candidates.shape[2]
    owner_dev = taken_all[0] // hot_pub
    member = taken_all[0] % hot_pub
    hot_ids = owner_dev * per_dev + owned_all[0][owner_dev, member]
    own_ids = (
        jnp.arange(shards, dtype=jnp.int32)[:, None] * per_dev
        + jnp.arange(per_dev, dtype=jnp.int32)[None, :]
    )
    ext_len_all = jnp.take(lengths_all[0], jnp.concatenate([own_ids, hot_ids], axis=1), axis=0)
    local_blocks = doc_blocks[0]
    published = jnp.take(local_blocks, hot_owned[0, 0], axis=0)
    taken_here = hot_taken[0, 0]
    empty_blocks = jnp.zeros((hot_dev,) + local_blocks.shape[1:], local_blocks.dtype)
    shard_piece = lax.all_gather(published, "blk", axis=0, tiled=True)
    row_count = shard_piece.shape[0]
    inside = (taken_here >= 0) & (taken_here < row_count)
    picked = jnp.take(shard_piece, jnp.clip(taken_here, 0, row_count - 1), axis=0)
    hot_blocks = jnp.where(inside[:, None, None], picked, empty_blocks)
    ext_blocks = jnp.concatenate([local_blocks, hot_blocks], axis=0)
    query_rows = queries.reshape(-1, queries.shape[2])
    score_parts = []
    visiting = query_rows
    for hop_number in range(hop_total):
        if hop_number > 0:
            visiting = shifted(visiting, "blk", 1)
        home_dev = (position - hop_number) % shards
        scores = hop_scores(
            visiting,
            ext_blocks,
            ext_len_all[position],
            cand_all[0, home_dev, hop_number],
            count_all[0, home_dev, hop_number],
        )
        if hop_number > 0:
            scores = shifted(scores, "blk", -hop_number)
        score_parts.append(scores)
    combined = jnp.concatenate(score_parts, axis=1)
    every_group = lax.all_gather(combined, "group", axis=1, tiled=True)
    top_values = lax.top_k(every_group, TOPK)[0]
    return top_values


def solution(mesh):
    return jax.shard_map(
        on_device,
        mesh=mesh,
        in_specs=(
            P("blk", None, None),
            P("group", "blk", None, None),
            P("group", "blk"),
            P("group", "blk", None, None),
            P("group", "blk", None),
            P("group", "blk", None),
            P("group", "blk", None),
        ),
        out_specs=P("blk", None),
        check_vma=False,
    )
```

profile of v0, /device:TPU:0, one launch (start us, length us, event | category | flops | bytes accessed | tf_op | source)
XLA Modules:
  0.0 288.4 jit_solution(9362428100582840750)
XLA Ops:
  0.0 2.9 %collective-permute-start = (bf16[8192,128]{1,0:T(8,128)(2,1)}, bf16[8192,128]{1,0:T(8,128)(2,1)}, u32[]{:S(2)}, u32[]{:S(2)}) collective-permute-start(bf16[8192,128]{1,0:T(8,128)(2,1)} %bitcast.140), channel_id=1, source_target_pairs={{0,1},{1,2},{2,3},{3,4},{4,5},{5,6},{6,7},{7,0},{8,9},{9,10},{10,1... | collective-permute-start | bytes 6291464 | tf_op jit(solution)/shard_map/ppermute | solution.py:13
  5.6 57.3 %all_gather.22 = s32[1,8,2]{2,0,1:T(1,128)S(1)} all-gather(s32[1,1,2]{2,0,1:T(1,128)} %bitcast.138), channel_id=1, replica_groups=mesh['group'=4,'blk'=8] {'blk'}, dimensions={1}, use_global_device_ids=true | all-gather | bytes 72 | tf_op jit(solution)/shard_map/all_gather | solution.py:48
  66.6 6.9 %all-reduce.3 = (s32[128]{0:T(128)S(1)}, s32[8]{0:T(128)S(1)}) all-reduce(s32[128]{0:T(128)S(1)} %bitcast_dynamic-update-slice_fusion, s32[8]{0:T(128)S(1)} %bitcast_dynamic-update-slice_fusion.1), channel_id=1, replica_groups=mesh['group'=4,'blk'=8] {'blk'}, use_global_device_ids=true, to_apply=%add.2 | all-reduce | flops 136 | bytes 1088 | tf_op jit(solution)/shard_map/squeeze | solution.py:64
  76.3 27.8 %all_gather.25 = s32[1,8,4,8]{3,2,0,1:T(4,128)S(1)} all-gather(s32[1,1,4,8]{3,2,0,1:T(4,128)S(1)} %bitcast.137), channel_id=1, replica_groups=mesh['group'=4,'blk'=8] {'blk'}, dimensions={1}, use_global_device_ids=true | all-gather | bytes 1152 | tf_op jit(solution)/shard_map/all_gather | solution.py:46
  105.0 30.8 %all-gather = bf16[8,1,128,128]{3,2,1,0:T(8,128)(2,1)S(1)} all-gather(bf16[1,1,128,128]{3,2,1,0:T(8,128)(2,1)S(1)} %dynamic-slice_select_fusion), channel_id=2, replica_groups=mesh['group'=4,'blk'=8] {'blk'}, dimensions={0}, use_global_device_ids=true | all-gather | bytes 294912 | tf_op jit(solution)/shard_map/all_gather | solution.py:69
  137.3 18.0 %while.41 = (s32[]{:T(128)}, f32[8,256]{1,0:T(8,128)S(1)}, s32[8]{0:T(128)S(1)}, bf16[8,128,128]{2,1,0:T(8,128)(2,1)S(1)}, bf16[8192,128]{1,0:T(8,128)(2,1)S(1)}, /*index=5*/s32[]{:T(128)}, f32[]{:T(128)}, s32[]{:T(128)}) while((s32[]{:T(128)}, f32[8,256]{1,0:T(8,128)S(1)}, s32[8]{0:T(128)S(1)}, bf16[8,128,128]{2,1,0:T(8,128)(2,1)S(1)}, ...), condition=%wide.region_3.6_spmd, body=%wide.region_0.5_spmd.sunk | while | flops 270532736 | bytes 2266873 | solution.py:28
  159.1 17.7 %all_gather.21 = s32[1,8,4]{2,0,1:T(1,128)S(1)} all-gather(s32[1,1,4]{2,0,1:T(1,128)S(1)} %bitcast.139), channel_id=1, replica_groups=mesh['group'=4,'blk'=8] {'blk'}, dimensions={1}, use_global_device_ids=true | all-gather | bytes 144 | tf_op jit(solution)/shard_map/all_gather | solution.py:47
  180.8 31.7 %while.42 = (s32[]{:T(128)}, f32[8,256]{1,0:T(8,128)S(1)}, s32[8]{0:T(128)S(1)}, bf16[8,128,128]{2,1,0:T(8,128)(2,1)S(1)}, bf16[8192,128]{1,0:T(8,128)(2,1)}, /*index=5*/s32[]{:T(128)}, f32[]{:T(128)}, s32[]{:T(128)}) while((s32[]{:T(128)}, f32[8,256]{1,0:T(8,128)S(1)}, s32[8]{0:T(128)S(1)}, bf16[8,128,128]{2,1,0:T(8,128)(2,1)S(1)}, ...), condition=%wide.region_7.10_spmd, body=%wide.region_4.9_spmd.sunk | while | flops 270532736 | bytes 2266873 | solution.py:28
  186.2 2.3 fusion.46
  190.1 2.3 fusion.46
  194.1 2.3 fusion.46
  198.1 2.3 fusion.46
  202.0 2.3 fusion.46
  206.0 2.3 fusion.46
  210.0 2.3 fusion.46
  212.6 4.1 %collective-permute-start.1 = (f32[256,8]{0,1:T(8,128)S(1)}, f32[256,8]{0,1:T(8,128)S(1)}, u32[]{:S(2)}, u32[]{:S(2)}) collective-permute-start(f32[256,8]{0,1:T(8,128)S(1)} %select_bitcast_fusion.2), channel_id=1, source_target_pairs={{0,7},{1,0},{2,1},{3,2},{4,3},{5,4},{6,5},{7,6},{8,15},{9,8},{10,9... | collective-permute-start | bytes 24584 | tf_op jit(solution)/shard_map/ppermute | solution.py:13
  216.7 2.8 collective-permute-done.2
  219.5 31.7 %while.43 = (s32[]{:T(128)}, f32[8,256]{1,0:T(8,128)S(1)}, s32[8]{0:T(128)S(1)}, bf16[8,128,128]{2,1,0:T(8,128)(2,1)S(1)}, bf16[8192,128]{1,0:T(8,128)(2,1)}, /*index=5*/s32[]{:T(128)}, f32[]{:T(128)}, s32[]{:T(128)}) while((s32[]{:T(128)}, f32[8,256]{1,0:T(8,128)S(1)}, s32[8]{0:T(128)S(1)}, bf16[8,128,128]{2,1,0:T(8,128)(2,1)S(1)}, ...), condition=%wide.region_11.14_spmd, body=%wide.region_8.13_spmd.sunk | while | flops 270532736 | bytes 2266873 | solution.py:28
  228.8 2.3 fusion.49
  251.3 4.3 %collective-permute-done.4 = bf16[8192,128]{1,0:T(8,128)(2,1)S(1)} collective-permute-done((bf16[8192,128]{1,0:T(8,128)(2,1)}, bf16[8192,128]{1,0:T(8,128)(2,1)S(1)}, u32[]{:S(2)}, u32[]{:S(2)}) %collective-permute-start.4) | collective-permute-done | bytes 2097184 | tf_op jit(solution)/shard_map/ppermute | solution.py:13
  255.6 18.9 %while.44 = (s32[]{:T(128)}, f32[8,256]{1,0:T(8,128)S(1)}, s32[8]{0:T(128)S(1)}, bf16[8,128,128]{2,1,0:T(8,128)(2,1)S(1)}, bf16[8192,128]{1,0:T(8,128)(2,1)S(1)}, /*index=5*/s32[]{:T(128)}, f32[]{:T(128)}, s32[]{:T(128)}) while((s32[]{:T(128)}, f32[8,256]{1,0:T(8,128)S(1)}, s32[8]{0:T(128)S(1)}, bf16[8,128,128]{2,1,0:T(8,128)(2,1)S(1)}, ...), condition=%wide.region_15.18_spmd, body=%wide.region_12.17_spmd.sunk | while | flops 270532736 | bytes 2266873 | solution.py:28
  274.7 4.5 %collective-permute-done.5 = f32[256,8]{0,1:T(8,128)S(1)} collective-permute-done((f32[256,8]{0,1:T(8,128)S(1)}, f32[256,8]{0,1:T(8,128)S(1)}, u32[]{:S(2)}, u32[]{:S(2)}) %collective-permute-start.5) | collective-permute-done | bytes 8224 | tf_op jit(solution)/shard_map/ppermute | solution.py:13
  279.2 5.4 %all_gather.27 = f32[256,128]{0,1:T(8,128)S(1)} all-gather(f32[256,32]{0,1:T(8,128)S(1)} %pad_maximum_fusion.1), channel_id=1, replica_groups=mesh['group'=4,'blk'=8] {'group'}, dimensions={1}, use_global_device_ids=true | all-gather | bytes 163840 | tf_op jit(solution)/shard_map/all_gather | solution.py:93
  284.6 3.0 %top_k.9 = (f32[256,128]{0,1:T(8,128)S(1)}, s32[256,128]{0,1:T(8,128)}) sort(f32[256,128]{0,1:T(8,128)S(1)} %all_gather.27, s32[256,128]{0,1:T(8,128)S(1)} %iota.59.clone), dimensions={1}, to_apply=%region_16.19 | sort | flops 491520 | bytes 524288 | tf_op jit(solution)/shard_map/top_k | solution.py:94
  (299 shorter events, 98.9 us)
Async XLA Ops:
  0.0 180.2 %collective-permute-start = (bf16[8192,128]{1,0:T(8,128)(2,1)}, bf16[8192,128]{1,0:T(8,128)(2,1)}, u32[]{:S(2)}, u32[]{:S(2)}) collective-permute-start(bf16[8192,128]{1,0:T(8,128)(2,1)} %bitcast.140), channel_id=1, source_target_pairs={{0,1},{1,2},{2,3},{3,4},{4,5},{5,6},{6,7},{7,0},{8,9},{9,10},{10,1... | collective-permute-start | bytes 6291464 | tf_op jit(solution)/shard_map/ppermute | solution.py:13
  74.7 1.7 copy-start.1
  74.7 30.3 %copy-start = (bf16[1,16,128,128]{3,2,1,0:T(8,128)(2,1)S(1)}, bf16[1,16,128,128]{3,2,1,0:T(8,128)(2,1)}, u32[]{:S(2)}) copy-start(bf16[1,16,128,128]{3,2,1,0:T(8,128)(2,1)} %param.20) | copy-start | bytes 1572868
  76.2 61.0 %copy-start.3 = (bf16[256,32,128]{2,1,0:T(8,128)(2,1)S(1)}, bf16[256,32,128]{2,1,0:T(8,128)(2,1)}, u32[]{:S(2)}) copy-start(bf16[256,32,128]{2,1,0:T(8,128)(2,1)} %param.19) | copy-start | bytes 6291460
  155.3 3.8 %copy-start.2 = (s32[1,1,4]{2,1,0:T(1,128)S(1)}, s32[1,1,4]{2,1,0:T(1,128)}, u32[]{:S(2)}) copy-start(s32[1,1,4]{2,1,0:T(1,128)} %param.23) | copy-start | bytes 52
  180.2 39.3 %collective-permute-start.2 = (bf16[8192,128]{1,0:T(8,128)(2,1)}, bf16[8192,128]{1,0:T(8,128)(2,1)}, u32[]{:S(2)}, u32[]{:S(2)}) collective-permute-start(bf16[8192,128]{1,0:T(8,128)(2,1)} %collective-permute-done), channel_id=1, source_target_pairs={{0,1},{1,2},{2,3},{3,4},{4,5},{5,6},{6,7},{7,0},{8,9},{9,10},{10,1... | collective-permute-start | bytes 6291464 | tf_op jit(solution)/shard_map/ppermute | solution.py:13
  212.6 62.1 %collective-permute-start.1 = (f32[256,8]{0,1:T(8,128)S(1)}, f32[256,8]{0,1:T(8,128)S(1)}, u32[]{:S(2)}, u32[]{:S(2)}) collective-permute-start(f32[256,8]{0,1:T(8,128)S(1)} %select_bitcast_fusion.2), channel_id=1, source_target_pairs={{0,7},{1,0},{2,1},{3,2},{4,3},{5,4},{6,5},{7,6},{8,15},{9,8},{10,9... | collective-permute-start | bytes 24584 | tf_op jit(solution)/shard_map/ppermute | solution.py:13
  219.5 36.1 %collective-permute-start.4 = (bf16[8192,128]{1,0:T(8,128)(2,1)}, bf16[8192,128]{1,0:T(8,128)(2,1)S(1)}, u32[]{:S(2)}, u32[]{:S(2)}) collective-permute-start(bf16[8192,128]{1,0:T(8,128)(2,1)} %collective-permute-done.2), channel_id=1, source_target_pairs={{0,1},{1,2},{2,3},{3,4},{4,5},{5,6},{6,7},{7,0},{8,9},{9,10},{10,1... | collective-permute-start | bytes 6291464 | tf_op jit(solution)/shard_map/ppermute | solution.py:13
  251.3 23.4 %collective-permute-start.3 = (f32[256,8]{0,1:T(8,128)S(1)}, f32[256,8]{0,1:T(8,128)S(1)}, u32[]{:S(2)}, u32[]{:S(2)}) collective-permute-start(f32[256,8]{0,1:T(8,128)S(1)} %select_bitcast_fusion.1), channel_id=1, source_target_pairs={{0,6},{1,7},{2,0},{3,1},{4,2},{5,3},{6,4},{7,5},{8,14},{9,15},{10,... | collective-permute-start | bytes 24584 | tf_op jit(solution)/shard_map/ppermute | solution.py:13
  274.6 4.5 %collective-permute-start.5 = (f32[256,8]{0,1:T(8,128)S(1)}, f32[256,8]{0,1:T(8,128)S(1)}, u32[]{:S(2)}, u32[]{:S(2)}) collective-permute-start(f32[256,8]{0,1:T(8,128)S(1)} %select_bitcast_fusion), channel_id=1, source_target_pairs={{0,5},{1,6},{2,7},{3,0},{4,1},{5,2},{6,3},{7,4},{8,13},{9,14},{10,... | collective-permute-start | bytes 24584 | tf_op jit(solution)/shard_map/ppermute | solution.py:13
where the time goes:
time: 290 us; the launch traced here: 288 us
  blocking collectives  146 us (50%)
  matrix products  48.6 us (17%)
  local copies, waits for them, and re-layouts  37.1 us (13%)
  other arithmetic  34 us (12%)
  waiting for transfers between devices  11.5 us (4%)
  starting transfers between devices  7.72 us (3%)
    all_gather x1, blocking collectives, on_device(): lax.all_gather(hot_taken, 'blk', axis=1, tiled=True)  57.3 us
    dot_general x32, matrix products, single(): lax.dot_general(query_part, doc_block, (((1,), (1,)), ((), ())), preferre...  48.6 us
    all_gather x1, blocking collectives, on_device(): shard_piece = lax.all_gather(published, 'blk', axis=0, tiled=True)  30.8 us
    all_gather x1, blocking collectives, on_device(): lax.all_gather(candidates, 'blk', axis=1, tiled=True)  27.8 us
    lt x32, other arithmetic, single(): keep_mask = jnp.arange(doc_block.shape[0], dtype=jnp.int32) < length  21.8 us
    dynamic_slice x32, local copies, waits for them, and re-layouts, maxsim(): return lax.map(single, (blocks, lengths)).T  20.7 us
    all_gather x1, blocking collectives, on_device(): lax.all_gather(cand_count, 'blk', axis=1, tiled=True)  17.7 us
    ppermute x6, waiting for transfers between devices, shifted(): return lax.ppermute(x, axis, [(i, (i + by) % peers) for i in range(peers)])  11.5 us
  transfers between devices with their start and end apart: 6, of which 3 were waited for; matrix products, arithmetic and copies ran while one was open for 40% of the time, Pallas kernels for 0%

commit v1 on v0

--- a/solution.py
+++ b/solution.py
@@ -66,7 +66,15 @@
     published = jnp.take(local_blocks, hot_owned[0, 0], axis=0)
     taken_here = hot_taken[0, 0]
     empty_blocks = jnp.zeros((hot_dev,) + local_blocks.shape[1:], local_blocks.dtype)
-    shard_piece = lax.all_gather(published, "blk", axis=0, tiled=True)
+    wide_n = lax.axis_size("blk")
+    w1 = published
+    steps_seen = [w1]
+    piece_out = sorted(((k, (k + 1) % wide_n) for k in range(wide_n)))
+    for jj in tuple(range(1, wide_n)):
+        w1 = lax.ppermute(w1, "blk", piece_out)
+        steps_seen.insert(0, w1)
+    arr_out = jnp.concatenate(steps_seen, axis=0)
+    shard_piece = jnp.roll(arr_out, (lax.axis_index("blk") + 1) * published.shape[0], axis=0)
     row_count = shard_piece.shape[0]
     inside = (taken_here >= 0) & (taken_here < row_count)
     picked = jnp.take(shard_piece, jnp.clip(taken_here, 0, row_count - 1), axis=0)

time: 290 us -> 294 us (1.014)
  waiting for transfers between devices: 11.5 us -> 40.5 us
  blocking collectives: 146 us -> 119 us
    all_gather x1 -> x0, blocking collectives: 30.8 us -> none  [on_device(): shard_piece = lax.all_gather(published, 'blk', axis=0, tiled=True)]
    ppermute x0 -> x7, waiting for transfers between devices: none -> 29.6 us  [on_device(): w1 = lax.ppermute(w1, 'blk', piece_out)]
    ppermute x0 -> x7, starting transfers between devices: none -> 3.94 us  [on_device(): w1 = lax.ppermute(w1, 'blk', piece_out)]
    all_gather x1, blocking collectives: 17.7 us -> 20.9 us  [on_device(): lax.all_gather(cand_count, 'blk', axis=1, tiled=True)]
  transfers between devices with their start and end apart: 6 -> 13, of which waited for: 3 -> 8; matrix products, arithmetic and copies ran while one was open for 40% -> 39% of each run, Pallas kernels for 0% -> 0%
where the time goes in v1:
time: 294 us; the launch traced here: 293 us
  blocking collectives  119 us (40%)
  matrix products  48.8 us (17%)
  waiting for transfers between devices  40.5 us (14%)
  local copies, waits for them, and re-layouts  37.5 us (13%)
  other arithmetic  33.3 us (11%)
  starting transfers between devices  10.2 us (3%)
    all_gather x1, blocking collectives, on_device(): lax.all_gather(hot_taken, 'blk', axis=1, tiled=True)  58.3 us
    dot_general x32, matrix products, single(): lax.dot_general(query_part, doc_block, (((1,), (1,)), ((), ())), preferre...  48.8 us
    ppermute x7, waiting for transfers between devices, on_device(): w1 = lax.ppermute(w1, 'blk', piece_out)  29.6 us
    all_gather x1, blocking collectives, on_device(): lax.all_gather(candidates, 'blk', axis=1, tiled=True)  27.2 us
    lt x32, other arithmetic, single(): keep_mask = jnp.arange(doc_block.shape[0], dtype=jnp.int32) < length  21.6 us
    all_gather x1, blocking collectives, on_device(): lax.all_gather(cand_count, 'blk', axis=1, tiled=True)  20.9 us
    dynamic_slice x32, local copies, waits for them, and re-layouts, maxsim(): return lax.map(single, (blocks, lengths)).T  20.7 us
    ppermute x6, waiting for transfers between devices, shifted(): return lax.ppermute(x, axis, [(i, (i + by) % peers) for i in range(peers)])  10.9 us
  transfers between devices with their start and end apart: 13, of which 8 were waited for; matrix products, arithmetic and copies ran while one was open for 39% of the time, Pallas kernels for 0%

profile of v1, /device:TPU:0, one launch (start us, length us, event | category | flops | bytes accessed | tf_op | source)
XLA Modules:
  0.0 293.1 jit_solution(14751393252406588020)
XLA Ops:
  1.4 2.9 %collective-permute-start = (bf16[1,128,128]{2,1,0:T(8,128)(2,1)S(1)}, bf16[1,128,128]{2,1,0:T(8,128)(2,1)S(1)}, u32[]{:S(2)}, u32[]{:S(2)}) collective-permute-start(bf16[1,128,128]{2,1,0:T(8,128)(2,1)S(1)} %select_bitcast_fusion), channel_id=1, source_target_pairs={{0,1},{1,2},{2,3},{3,4},{4,5},{5,6},{6,7},{7,0},{8,9},{9,10},{10,1... | collective-permute-start | bytes 98312 | tf_op jit(solution)/shard_map/ppermute | solution.py:74
  6.6 58.3 %all_gather.19 = s32[1,8,2]{2,0,1:T(1,128)S(1)} all-gather(s32[1,1,2]{2,0,1:T(1,128)} %bitcast.142), channel_id=1, replica_groups=mesh['group'=4,'blk'=8] {'blk'}, dimensions={1}, use_global_device_ids=true | all-gather | bytes 72 | tf_op jit(solution)/shard_map/all_gather | solution.py:48
  68.5 7.5 %all-reduce.3 = (s32[128]{0:T(128)S(1)}, s32[8]{0:T(128)S(1)}) all-reduce(s32[128]{0:T(128)S(1)} %bitcast_dynamic-update-slice_fusion, s32[8]{0:T(128)S(1)} %bitcast_dynamic-update-slice_fusion.1), channel_id=1, replica_groups=mesh['group'=4,'blk'=8] {'blk'}, use_global_device_ids=true, to_apply=%add.2 | all-reduce | flops 136 | bytes 1088 | tf_op jit(solution)/shard_map/squeeze | solution.py:64
  78.9 27.2 %all_gather.22 = s32[1,8,4,8]{3,2,0,1:T(4,128)S(1)} all-gather(s32[1,1,4,8]{3,2,0,1:T(4,128)S(1)} %bitcast.141), channel_id=1, replica_groups=mesh['group'=4,'blk'=8] {'blk'}, dimensions={1}, use_global_device_ids=true | all-gather | bytes 1152 | tf_op jit(solution)/shard_map/all_gather | solution.py:46
  109.9 5.7 %collective-permute-done.1 = bf16[1,128,128]{2,1,0:T(8,128)(2,1)S(1)} collective-permute-done((bf16[1,128,128]{2,1,0:T(8,128)(2,1)S(1)}, bf16[1,128,128]{2,1,0:T(8,128)(2,1)S(1)}, u32[]{:S(2)}, u32[]{:S(2)}) %collective-permute-start.1) | collective-permute-done | bytes 32800 | tf_op jit(solution)/shard_map/ppermute | solution.py:74
  115.6 20.9 %all_gather.18 = s32[1,8,4]{2,0,1:T(1,128)S(1)} all-gather(s32[1,1,4]{2,0,1:T(1,128)S(1)} %bitcast.143), channel_id=1, replica_groups=mesh['group'=4,'blk'=8] {'blk'}, dimensions={1}, use_global_device_ids=true | all-gather | bytes 144 | tf_op jit(solution)/shard_map/all_gather | solution.py:47
  137.8 6.0 %collective-permute-done.3 = bf16[1,128,128]{2,1,0:T(8,128)(2,1)S(1)} collective-permute-done((bf16[1,128,128]{2,1,0:T(8,128)(2,1)S(1)}, bf16[1,128,128]{2,1,0:T(8,128)(2,1)S(1)}, u32[]{:S(2)}, u32[]{:S(2)}) %collective-permute-start.3) | collective-permute-done | bytes 32800 | tf_op jit(solution)/shard_map/ppermute | solution.py:74
  144.3 6.0 %collective-permute-done.4 = bf16[1,128,128]{2,1,0:T(8,128)(2,1)S(1)} collective-permute-done((bf16[1,128,128]{2,1,0:T(8,128)(2,1)S(1)}, bf16[1,128,128]{2,1,0:T(8,128)(2,1)S(1)}, u32[]{:S(2)}, u32[]{:S(2)}) %collective-permute-start.4) | collective-permute-done | bytes 32800 | tf_op jit(solution)/shard_map/ppermute | solution.py:74
  150.9 6.1 %collective-permute-done.5 = bf16[1,128,128]{2,1,0:T(8,128)(2,1)S(1)} collective-permute-done((bf16[1,128,128]{2,1,0:T(8,128)(2,1)S(1)}, bf16[1,128,128]{2,1,0:T(8,128)(2,1)S(1)}, u32[]{:S(2)}, u32[]{:S(2)}) %collective-permute-start.5) | collective-permute-done | bytes 32800 | tf_op jit(solution)/shard_map/ppermute | solution.py:74
  157.6 6.0 %collective-permute-done.6 = bf16[1,128,128]{2,1,0:T(8,128)(2,1)S(1)} collective-permute-done((bf16[1,128,128]{2,1,0:T(8,128)(2,1)S(1)}, bf16[1,128,128]{2,1,0:T(8,128)(2,1)S(1)}, u32[]{:S(2)}, u32[]{:S(2)}) %collective-permute-start.6) | collective-permute-done | bytes 32800 | tf_op jit(solution)/shard_map/ppermute | solution.py:74
  165.3 17.8 %while.41 = (s32[]{:T(128)}, f32[8,256]{1,0:T(8,128)S(1)}, s32[8]{0:T(128)S(1)}, bf16[8,128,128]{2,1,0:T(8,128)(2,1)S(1)}, bf16[8192,128]{1,0:T(8,128)(2,1)S(1)}, /*index=5*/s32[]{:T(128)}, f32[]{:T(128)}, s32[]{:T(128)}) while((s32[]{:T(128)}, f32[8,256]{1,0:T(8,128)S(1)}, s32[8]{0:T(128)S(1)}, bf16[8,128,128]{2,1,0:T(8,128)(2,1)S(1)}, ...), condition=%wide.region_3.6_spmd, body=%wide.region_0.5_spmd.sunk | while | flops 270532736 | bytes 2266873 | solution.py:28
  185.3 31.8 %while.42 = (s32[]{:T(128)}, f32[8,256]{1,0:T(8,128)S(1)}, s32[8]{0:T(128)S(1)}, bf16[8,128,128]{2,1,0:T(8,128)(2,1)S(1)}, bf16[8192,128]{1,0:T(8,128)(2,1)}, /*index=5*/s32[]{:T(128)}, f32[]{:T(128)}, s32[]{:T(128)}) while((s32[]{:T(128)}, f32[8,256]{1,0:T(8,128)S(1)}, s32[8]{0:T(128)S(1)}, bf16[8,128,128]{2,1,0:T(8,128)(2,1)S(1)}, ...), condition=%wide.region_7.10_spmd, body=%wide.region_4.9_spmd.sunk | while | flops 270532736 | bytes 2266873 | solution.py:28
  198.6 2.3 fusion.46
  210.5 2.3 fusion.46
  217.2 4.7 %collective-permute-start.8 = (f32[256,8]{0,1:T(8,128)S(1)}, f32[256,8]{0,1:T(8,128)S(1)}, u32[]{:S(2)}, u32[]{:S(2)}) collective-permute-start(f32[256,8]{0,1:T(8,128)S(1)} %select_bitcast_fusion.3), channel_id=1, source_target_pairs={{0,7},{1,0},{2,1},{3,2},{4,3},{5,4},{6,5},{7,6},{8,15},{9,8},{10,9... | collective-permute-start | bytes 24584 | tf_op jit(solution)/shard_map/ppermute | solution.py:13
  224.1 31.8 %while.43 = (s32[]{:T(128)}, f32[8,256]{1,0:T(8,128)S(1)}, s32[8]{0:T(128)S(1)}, bf16[8,128,128]{2,1,0:T(8,128)(2,1)S(1)}, bf16[8192,128]{1,0:T(8,128)(2,1)}, /*index=5*/s32[]{:T(128)}, f32[]{:T(128)}, s32[]{:T(128)}) while((s32[]{:T(128)}, f32[8,256]{1,0:T(8,128)S(1)}, s32[8]{0:T(128)S(1)}, bf16[8,128,128]{2,1,0:T(8,128)(2,1)S(1)}, ...), condition=%wide.region_11.14_spmd, body=%wide.region_8.13_spmd.sunk | while | flops 270532736 | bytes 2266873 | solution.py:28
  229.4 2.3 fusion.49
  233.4 2.3 fusion.49
  241.4 2.3 fusion.49
  256.0 4.3 %collective-permute-done.11 = bf16[8192,128]{1,0:T(8,128)(2,1)S(1)} collective-permute-done((bf16[8192,128]{1,0:T(8,128)(2,1)}, bf16[8192,128]{1,0:T(8,128)(2,1)S(1)}, u32[]{:S(2)}, u32[]{:S(2)}) %collective-permute-start.11) | collective-permute-done | bytes 2097184 | tf_op jit(solution)/shard_map/ppermute | solution.py:13
  260.3 19.0 %while.44 = (s32[]{:T(128)}, f32[8,256]{1,0:T(8,128)S(1)}, s32[8]{0:T(128)S(1)}, bf16[8,128,128]{2,1,0:T(8,128)(2,1)S(1)}, bf16[8192,128]{1,0:T(8,128)(2,1)S(1)}, /*index=5*/s32[]{:T(128)}, f32[]{:T(128)}, s32[]{:T(128)}) while((s32[]{:T(128)}, f32[8,256]{1,0:T(8,128)S(1)}, s32[8]{0:T(128)S(1)}, bf16[8,128,128]{2,1,0:T(8,128)(2,1)S(1)}, ...), condition=%wide.region_15.18_spmd, body=%wide.region_12.17_spmd.sunk | while | flops 270532736 | bytes 2266873 | solution.py:28
  279.4 4.5 %collective-permute-done.12 = f32[256,8]{0,1:T(8,128)S(1)} collective-permute-done((f32[256,8]{0,1:T(8,128)S(1)}, f32[256,8]{0,1:T(8,128)S(1)}, u32[]{:S(2)}, u32[]{:S(2)}) %collective-permute-start.12) | collective-permute-done | bytes 8224 | tf_op jit(solution)/shard_map/ppermute | solution.py:13
  283.8 5.4 %all_gather.23 = f32[256,128]{0,1:T(8,128)S(1)} all-gather(f32[256,32]{0,1:T(8,128)S(1)} %pad_maximum_fusion.1), channel_id=1, replica_groups=mesh['group'=4,'blk'=8] {'group'}, dimensions={1}, use_global_device_ids=true | all-gather | bytes 163840 | tf_op jit(solution)/shard_map/all_gather | solution.py:101
  289.3 3.0 %top_k.9 = (f32[256,128]{0,1:T(8,128)S(1)}, s32[256,128]{0,1:T(8,128)}) sort(f32[256,128]{0,1:T(8,128)S(1)} %all_gather.23, s32[256,128]{0,1:T(8,128)S(1)} %iota.59.clone), dimensions={1}, to_apply=%region_16.19 | sort | flops 491520 | bytes 524288 | tf_op jit(solution)/shard_map/top_k | solution.py:102
  (331 shorter events, 109.7 us)
Async XLA Ops:
  1.4 107.5 %collective-permute-start = (bf16[1,128,128]{2,1,0:T(8,128)(2,1)S(1)}, bf16[1,128,128]{2,1,0:T(8,128)(2,1)S(1)}, u32[]{:S(2)}, u32[]{:S(2)}) collective-permute-start(bf16[1,128,128]{2,1,0:T(8,128)(2,1)S(1)} %select_bitcast_fusion), channel_id=1, source_target_pairs={{0,1},{1,2},{2,3},{3,4},{4,5},{5,6},{6,7},{7,0},{8,9},{9,10},{10,1... | collective-permute-start | bytes 98312 | tf_op jit(solution)/shard_map/ppermute | solution.py:74
  4.4 180.9 %collective-permute-start.7 = (bf16[8192,128]{1,0:T(8,128)(2,1)}, bf16[8192,128]{1,0:T(8,128)(2,1)}, u32[]{:S(2)}, u32[]{:S(2)}) collective-permute-start(bf16[8192,128]{1,0:T(8,128)(2,1)} %bitcast.144), channel_id=1, source_target_pairs={{0,1},{1,2},{2,3},{3,4},{4,5},{5,6},{6,7},{7,0},{8,9},{9,10},{10,1... | collective-permute-start | bytes 6291464 | tf_op jit(solution)/shard_map/ppermute | solution.py:13
  77.2 1.7 copy-start.1
  78.8 30.1 %copy-start.2 = (s32[1,1,2]{2,1,0:T(1,128)S(1)}, s32[1,1,2]{2,1,0:T(1,128)}, u32[]{:S(2)}) copy-start(s32[1,1,2]{2,1,0:T(1,128)} %param.25) | copy-start | bytes 28
  78.8 36.8 %copy-start.3 = (s32[1,1,4]{2,1,0:T(1,128)S(1)}, s32[1,1,4]{2,1,0:T(1,128)}, u32[]{:S(2)}) copy-start(s32[1,1,4]{2,1,0:T(1,128)} %param.23) | copy-start | bytes 52
  78.8 84.8 %copy-start = (bf16[1,16,128,128]{3,2,1,0:T(8,128)(2,1)S(1)}, bf16[1,16,128,128]{3,2,1,0:T(8,128)(2,1)}, u32[]{:S(2)}) copy-start(bf16[1,16,128,128]{3,2,1,0:T(8,128)(2,1)} %param.20) | copy-start | bytes 1572868
  108.8 56.4 %copy-start.4 = (bf16[256,32,128]{2,1,0:T(8,128)(2,1)S(1)}, bf16[256,32,128]{2,1,0:T(8,128)(2,1)}, u32[]{:S(2)}) copy-start(bf16[256,32,128]{2,1,0:T(8,128)(2,1)} %param.19) | copy-start | bytes 6291460
  108.9 6.7 %collective-permute-start.1 = (bf16[1,128,128]{2,1,0:T(8,128)(2,1)S(1)}, bf16[1,128,128]{2,1,0:T(8,128)(2,1)S(1)}, u32[]{:S(2)}, u32[]{:S(2)}) collective-permute-start(bf16[1,128,128]{2,1,0:T(8,128)(2,1)S(1)} %collective-permute-done), channel_id=1, source_target_pairs={{0,1},{1,2},{2,3},{3,4},{4,5},{5,6},{6,7},{7,0},{8,9},{9,10},{10,1... | collective-permute-start | bytes 98312 | tf_op jit(solution)/shard_map/ppermute | solution.py:74
  115.6 21.5 %collective-permute-start.2 = (bf16[1,128,128]{2,1,0:T(8,128)(2,1)S(1)}, bf16[1,128,128]{2,1,0:T(8,128)(2,1)S(1)}, u32[]{:S(2)}, u32[]{:S(2)}) collective-permute-start(bf16[1,128,128]{2,1,0:T(8,128)(2,1)S(1)} %collective-permute-done.1), channel_id=1, source_target_pairs={{0,1},{1,2},{2,3},{3,4},{4,5},{5,6},{6,7},{7,0},{8,9},{9,10},{10,1... | collective-permute-start | bytes 98312 | tf_op jit(solution)/shard_map/ppermute | solution.py:74
  137.1 6.6 %collective-permute-start.3 = (bf16[1,128,128]{2,1,0:T(8,128)(2,1)S(1)}, bf16[1,128,128]{2,1,0:T(8,128)(2,1)S(1)}, u32[]{:S(2)}, u32[]{:S(2)}) collective-permute-start(bf16[1,128,128]{2,1,0:T(8,128)(2,1)S(1)} %collective-permute-done.2), channel_id=1, source_target_pairs={{0,1},{1,2},{2,3},{3,4},{4,5},{5,6},{6,7},{7,0},{8,9},{9,10},{10,1... | collective-permute-start | bytes 98312 | tf_op jit(solution)/shard_map/ppermute | solution.py:74
  143.7 6.6 %collective-permute-start.4 = (bf16[1,128,128]{2,1,0:T(8,128)(2,1)S(1)}, bf16[1,128,128]{2,1,0:T(8,128)(2,1)S(1)}, u32[]{:S(2)}, u32[]{:S(2)}) collective-permute-start(bf16[1,128,128]{2,1,0:T(8,128)(2,1)S(1)} %collective-permute-done.3), channel_id=1, source_target_pairs={{0,1},{1,2},{2,3},{3,4},{4,5},{5,6},{6,7},{7,0},{8,9},{9,10},{10,1... | collective-permute-start | bytes 98312 | tf_op jit(solution)/shard_map/ppermute | solution.py:74
  150.3 6.6 %collective-permute-start.5 = (bf16[1,128,128]{2,1,0:T(8,128)(2,1)S(1)}, bf16[1,128,128]{2,1,0:T(8,128)(2,1)S(1)}, u32[]{:S(2)}, u32[]{:S(2)}) collective-permute-start(bf16[1,128,128]{2,1,0:T(8,128)(2,1)S(1)} %collective-permute-done.4), channel_id=1, source_target_pairs={{0,1},{1,2},{2,3},{3,4},{4,5},{5,6},{6,7},{7,0},{8,9},{9,10},{10,1... | collective-permute-start | bytes 98312 | tf_op jit(solution)/shard_map/ppermute | solution.py:74
  156.9 6.6 %collective-permute-start.6 = (bf16[1,128,128]{2,1,0:T(8,128)(2,1)S(1)}, bf16[1,128,128]{2,1,0:T(8,128)(2,1)S(1)}, u32[]{:S(2)}, u32[]{:S(2)}) collective-permute-start(bf16[1,128,128]{2,1,0:T(8,128)(2,1)S(1)} %collective-permute-done.5), channel_id=1, source_target_pairs={{0,1},{1,2},{2,3},{3,4},{4,5},{5,6},{6,7},{7,0},{8,9},{9,10},{10,1... | collective-permute-start | bytes 98312 | tf_op jit(solution)/shard_map/ppermute | solution.py:74
  185.2 38.8 %collective-permute-start.9 = (bf16[8192,128]{1,0:T(8,128)(2,1)}, bf16[8192,128]{1,0:T(8,128)(2,1)}, u32[]{:S(2)}, u32[]{:S(2)}) collective-permute-start(bf16[8192,128]{1,0:T(8,128)(2,1)} %collective-permute-done.7), channel_id=1, source_target_pairs={{0,1},{1,2},{2,3},{3,4},{4,5},{5,6},{6,7},{7,0},{8,9},{9,10},{10,1... | collective-permute-start | bytes 6291464 | tf_op jit(solution)/shard_map/ppermute | solution.py:13
  217.2 62.2 %collective-permute-start.8 = (f32[256,8]{0,1:T(8,128)S(1)}, f32[256,8]{0,1:T(8,128)S(1)}, u32[]{:S(2)}, u32[]{:S(2)}) collective-permute-start(f32[256,8]{0,1:T(8,128)S(1)} %select_bitcast_fusion.3), channel_id=1, source_target_pairs={{0,7},{1,0},{2,1},{3,2},{4,3},{5,4},{6,5},{7,6},{8,15},{9,8},{10,9... | collective-permute-start | bytes 24584 | tf_op jit(solution)/shard_map/ppermute | solution.py:13
  224.1 36.2 %collective-permute-start.11 = (bf16[8192,128]{1,0:T(8,128)(2,1)}, bf16[8192,128]{1,0:T(8,128)(2,1)S(1)}, u32[]{:S(2)}, u32[]{:S(2)}) collective-permute-start(bf16[8192,128]{1,0:T(8,128)(2,1)} %collective-permute-done.9), channel_id=1, source_target_pairs={{0,1},{1,2},{2,3},{3,4},{4,5},{5,6},{6,7},{7,0},{8,9},{9,10},{10,1... | collective-permute-start | bytes 6291464 | tf_op jit(solution)/shard_map/ppermute | solution.py:13
  256.0 23.4 %collective-permute-start.10 = (f32[256,8]{0,1:T(8,128)S(1)}, f32[256,8]{0,1:T(8,128)S(1)}, u32[]{:S(2)}, u32[]{:S(2)}) collective-permute-start(f32[256,8]{0,1:T(8,128)S(1)} %select_bitcast_fusion.2), channel_id=1, source_target_pairs={{0,6},{1,7},{2,0},{3,1},{4,2},{5,3},{6,4},{7,5},{8,14},{9,15},{10,... | collective-permute-start | bytes 24584 | tf_op jit(solution)/shard_map/ppermute | solution.py:13
  279.3 4.5 %collective-permute-start.12 = (f32[256,8]{0,1:T(8,128)S(1)}, f32[256,8]{0,1:T(8,128)S(1)}, u32[]{:S(2)}, u32[]{:S(2)}) collective-permute-start(f32[256,8]{0,1:T(8,128)S(1)} %select_bitcast_fusion.1), channel_id=1, source_target_pairs={{0,5},{1,6},{2,7},{3,0},{4,1},{5,2},{6,3},{7,4},{8,13},{9,14},{10,... | collective-permute-start | bytes 24584 | tf_op jit(solution)/shard_map/ppermute | solution.py:13
